TPU v7x, 256 devices: a whole 4x4x8 slice. The times are simulated.
256 devices in a mesh: row: 8 (over y_hi, x), col: 32 (over y_lo, z, core).
Axes of the slice: x: 4, y: 4 (y_hi: 2, y_lo: 2; y = y_hi * 2 + y_lo), z: 8, core: 2. Of those that a mesh axis runs over, the one named last changes fastest.
Arguments:
- messages: bfloat16 [8, 32, 1024, 512], P('row', 'col'), may hold values from -6 to 6
- targets: int32 [8, 32, 1024], P('row', 'col'), may hold values from 0 to 511
- reverse_rows: int32 [8, 32, 8, 128], P('row', 'col'), may hold values from 0 to 127, as said below
- nodes: bfloat16 [32, 512, 512], P('col', 'row'), may hold values from -6 to 6
- w_in: bfloat16 [2, 1536, 512], replicated, may hold values from -0.15625 to 0.15625
- w_res: bfloat16 [2, 2, 2, 512, 512], replicated, may hold values from -0.25 to 0.25
- w_node: bfloat16 [2, 512, 512], replicated, may hold values from -0.25 to 0.25
Outputs:
- edge_out: bfloat16 [8, 32, 1024, 512], P('row', 'col')
- node_out: bfloat16 [32, 512, 512], P('col', 'row')
Inputs may be any that keep to these rules, and one draw needn't show every extreme that they name: reverse_rows[s, c, k] is a permutation of the block's rows, and the reversal is an involution: the reversed edge of the reversed edge is the edge itself.
All inputs are finite; a program needn't handle non-finite values.
Results may differ from a plain program's by a relative error of at most 0.0065.
Values may be sent and summed in bfloat16 or wider, within the bound.
A program may use at most 64 MiB of HBM per device.

v0:
```python
import functools
import math

import jax
import jax.numpy as jnp
from jax import lax
from jax.experimental import pallas as pl
from jax.experimental.pallas import tpu as pltpu
from jax.sharding import PartitionSpec as P

OFFSETS = (0, 0, 1, -1, 2, -2, 3, -3)
ROOT_HALF = 0.7071067811865476
MESH = pl.DeviceIdType.MESH
F32 = jnp.float32
BF16 = jnp.bfloat16


def silu(v):
    half = 0.5 * v
    return half + half * jnp.tanh(half)


def mm(a, b):
    return jnp.dot(a, b, preferred_element_type=F32)


def kernel(
    rows_n,
    cols_n,
    msg,
    tgt,
    rev,
    node,
    w_in_hbm,
    w_res_hbm,
    w_node_hbm,
    edge_out,
    node_out,
    w_in,
    w_res,
    w_node,
    cur,
    onehot,
    perm,
    base,
    own_part,
    h_tgt,
    pre,
    h_own,
    h_all,
    part_out,
    part_in,
    u_out,
    u_in,
    w_sem,
    rs_send,
    rs_recv,
    ag_send,
    ag_recv,
    col_send,
    col_recv,
    out_sem,
):
    r, c = lax.axis_index("row"), lax.axis_index("col")
    edges, feat = msg.shape
    share = node.shape[0]
    points = share * rows_n
    block = edges // len(OFFSETS)
    pair = 2 * block
    agg_scale = 1.0 / math.sqrt(edges // share)
    layers = w_in_hbm.shape[0]

    def row_peer(j):
        return lax.rem(r + j, rows_n)

    def col_peer(offset):
        return lax.rem(c + offset + cols_n, cols_n)

    barrier = pltpu.get_barrier_semaphore()
    for j in range(1, rows_n):
        pl.semaphore_signal(barrier, inc=1, device_id=(row_peer(j), c), device_id_type=MESH)
    for off in OFFSETS[2:]:
        pl.semaphore_signal(barrier, inc=1, device_id=(r, col_peer(off)), device_id_type=MESH)

    loads = []
    for t in range(layers):
        for i, (src, dst) in enumerate(
            ((w_in_hbm, w_in), (w_node_hbm, w_node), (w_res_hbm, w_res))
        ):
            loads.append(pltpu.make_async_copy(src.at[t], dst.at[t], w_sem.at[t, i]))
            loads[-1].start()

    def rs_copy(t, j):
        return pltpu.make_async_remote_copy(
            src_ref=part_out.at[t, j - 1],
            dst_ref=part_in.at[t, j - 1],
            send_sem=rs_send.at[t, j - 1],
            recv_sem=rs_recv.at[t, j - 1],
            device_id=(row_peer(j), c),
            device_id_type=MESH,
        )

    def ag_copy(t, j):
        mine = pl.ds(pl.multiple_of(r * share, share), share)
        return pltpu.make_async_remote_copy(
            src_ref=h_all.at[t, mine],
            dst_ref=h_all.at[t, mine],
            send_sem=ag_send.at[t, j - 1],
            recv_sem=ag_recv.at[t, j - 1],
            device_id=(row_peer(j), c),
            device_id_type=MESH,
        )

    def ag_arrival(t, j):
        theirs = pl.ds(pl.multiple_of(row_peer(rows_n - j) * share, share), share)
        return pltpu.make_async_remote_copy(
            src_ref=h_all.at[t, theirs],
            dst_ref=h_all.at[t, theirs],
            send_sem=ag_send.at[t, j - 1],
            recv_sem=ag_recv.at[t, j - 1],
            device_id=(row_peer(j), c),
            device_id_type=MESH,
        )

    def col_copy(t, b):
        return pltpu.make_async_remote_copy(
            src_ref=u_out.at[t, b],
            dst_ref=u_in.at[t, (b ^ 1) - 2],
            send_sem=col_send.at[t, b - 2],
            recv_sem=col_recv.at[t, (b ^ 1) - 2],
            device_id=(r, col_peer(OFFSETS[b])),
            device_id_type=MESH,
        )

    def col_arrival(t, k):
        return pltpu.make_async_remote_copy(
            src_ref=u_out.at[t, k],
            dst_ref=u_in.at[t, k - 2],
            send_sem=col_send.at[t, k - 2],
            recv_sem=col_recv.at[t, k - 2],
            device_id=(r, col_peer(OFFSETS[k])),
            device_id_type=MESH,
        )

    def send_parts(t, messages):
        half = points // 2
        per = rows_n // 2
        for part in range(2):
            first = lax.rem(r + 1 + part * per, rows_n) * share
            ids = lax.rem(lax.broadcasted_iota(jnp.int32, (half, edges), 0) + first, points)
            hot = jnp.where(tgt[...] == ids, 1.0, 0.0).astype(BF16)
            sums = mm(hot, messages[...])
            for i in range(per):
                j = part * per + i + 1
                rows = sums[i * share : (i + 1) * share]
                if j == rows_n:
                    own_part[...] = rows
                    continue
                part_out[t, j - 1] = rows.astype(BF16)
                if t == 0 and j == 1:
                    pl.semaphore_wait(barrier, rows_n - 1 + len(OFFSETS) - 2)
                rs_copy(t, j).start()

    send_parts(0, msg)

    lane = lax.broadcasted_iota(jnp.int32, (block, block), 1)
    for k in range(len(OFFSETS)):
        rows = pl.ds(k * block, block)
        ids = jnp.broadcast_to(tgt[0:1, k * block : (k + 1) * block], (block, block)).T
        for i in range(points // block):
            onehot[rows, i * block : (i + 1) * block] = jnp.where(
                ids == lane + i * block, 1.0, 0.0
            ).astype(BF16)
        ids = jnp.broadcast_to(rev[k : k + 1, :], (block, block)).T
        perm[k] = jnp.where(ids == lane, 1.0, 0.0).astype(BF16)

    h_own[...] = node[...]
    for t in range(layers):
        last = t == layers - 1
        held = msg if t == 0 else cur
        loads[3 * t].wait()
        for q in range(edges // pair):
            rows = pl.ds(q * pair, pair)
            base[rows] = mm(held[rows], w_in[t, :feat])

        loads[3 * t + 1].wait()
        total = own_part[...]
        for j in range(1, rows_n):
            rs_copy(t, j).wait_recv()
            total = total + part_in[t, j - 1].astype(F32)
        scaled = (total * agg_scale).astype(BF16)
        h_new = (h_own[...].astype(F32) + silu(mm(scaled, w_node[t]))).astype(BF16)
        h_own[...] = h_new
        h_all[t, pl.ds(pl.multiple_of(r * share, share), share)] = h_new
        for j in range(1, rows_n):
            ag_copy(t, j).start()
        if last:
            node_copy = pltpu.make_async_copy(h_own, node_out, out_sem.at[edges // pair])
            node_copy.start()
        for j in range(1, rows_n):
            ag_arrival(t, j).wait_recv()

        for q in (3, 2, 1, 0):
            rows = pl.ds(q * pair, pair)
            picked = mm(onehot[rows], h_all[t]).astype(BF16)
            h_tgt[rows] = picked
            u = (base[rows] + mm(picked, w_in[t, feat : 2 * feat])).astype(BF16)
            for i in range(2):
                b = 2 * q + i
                u_out[t, b] = u[i * block : (i + 1) * block]
                if q:
                    col_copy(t, b).start()
        for q in (0, 1, 2, 3):
            rows = pl.ds(q * pair, pair)
            pre[rows] = mm(h_tgt[rows], w_in[t, 2 * feat :])

        loads[3 * t + 2].wait()
        for q in (0, 1, 2, 3):
            rows = pl.ds(q * pair, pair)
            moved = []
            for k in (2 * q, 2 * q + 1):
                if q:
                    col_arrival(t, k).wait_recv()
                    moved.append(mm(perm[k], u_in[t, k - 2]))
                else:
                    moved.append(mm(perm[k], u_out[t, k ^ 1]))
            hidden = silu(pre[rows] + jnp.concatenate(moved, axis=0)).astype(BF16)
            inner = silu(mm(hidden, w_res[t, 0, 0])).astype(BF16)
            hidden = (
                (hidden.astype(F32) + silu(mm(inner, w_res[t, 0, 1]))) * ROOT_HALF
            ).astype(BF16)
            inner = silu(mm(hidden, w_res[t, 1, 0])).astype(BF16)
            summed = (hidden.astype(F32) + silu(mm(inner, w_res[t, 1, 1]))) * ROOT_HALF
            cur[rows] = ((held[rows].astype(F32) + summed) * ROOT_HALF).astype(BF16)
            if last:
                pltpu.make_async_copy(cur.at[rows], edge_out.at[rows], out_sem.at[q]).start()
        if not last:
            send_parts(t + 1, cur)

    for t in range(layers):
        for j in range(1, rows_n):
            rs_copy(t, j).wait_send()
            ag_copy(t, j).wait_send()
        for b in range(2, len(OFFSETS)):
            col_copy(t, b).wait_send()
    for q in range(edges // pair):
        rows = pl.ds(q * pair, pair)
        pltpu.make_async_copy(cur.at[rows], edge_out.at[rows], out_sem.at[q]).wait()
    node_copy.wait()


def shards(rows_n, cols_n, messages, targets, reverse_rows, nodes, w_in, w_res, w_node):
    msg, tgt, rev, node = messages[0, 0], targets[0], reverse_rows[0, 0], nodes[0]
    edges, feat = msg.shape
    share = node.shape[0]
    points = share * rows_n
    layers = w_in.shape[0]
    blocks = len(OFFSETS)
    block = edges // blocks
    dma = pltpu.SemaphoreType.DMA
    vmem = pl.BlockSpec(memory_space=pltpu.VMEM)
    hbm = pl.BlockSpec(memory_space=pl.ANY)
    edge_out, node_out = pl.pallas_call(
        functools.partial(kernel, rows_n, cols_n),
        out_shape=(
            jax.ShapeDtypeStruct((edges, feat), BF16),
            jax.ShapeDtypeStruct((share, feat), BF16),
        ),
        in_specs=[vmem] * 4 + [hbm] * 3,
        out_specs=(hbm, hbm),
        scratch_shapes=[
            pltpu.VMEM(w_in.shape, BF16),
            pltpu.VMEM(w_res.shape, BF16),
            pltpu.VMEM(w_node.shape, BF16),
            pltpu.VMEM((edges, feat), BF16),
            pltpu.VMEM((edges, points), BF16),
            pltpu.VMEM((blocks, block, block), BF16),
            pltpu.VMEM((edges, feat), F32),
            pltpu.VMEM((share, feat), F32),
            pltpu.VMEM((edges, feat), BF16),
            pltpu.VMEM((edges, feat), F32),
            pltpu.VMEM((share, feat), BF16),
            pltpu.VMEM((layers, points, feat), BF16),
            pltpu.VMEM((layers, rows_n - 1, share, feat), BF16),
            pltpu.VMEM((layers, rows_n - 1, share, feat), BF16),
            pltpu.VMEM((layers, blocks, block, feat), BF16),
            pltpu.VMEM((layers, blocks - 2, block, feat), BF16),
            dma((layers, 3)),
            dma((layers, rows_n - 1)),
            dma((layers, rows_n - 1)),
            dma((layers, rows_n - 1)),
            dma((layers, rows_n - 1)),
            dma((layers, blocks - 2)),
            dma((layers, blocks - 2)),
            dma((blocks // 2 + 1,)),
        ],
        compiler_params=pltpu.CompilerParams(
            collective_id=0, has_side_effects=True, vmem_limit_bytes=56 * 2**20
        ),
        cost_estimate=pl.CostEstimate(
            flops=11 * 10**9, bytes_accessed=12 * 10**6, transcendentals=5 * 10**6
        ),
    )(msg, tgt, rev, node, w_in, w_res, w_node)
    return edge_out[None, None], node_out[None]


def solution(mesh):
    in_specs = (
        P("row", "col", None, None),
        P("row", "col", None),
        P("row", "col", None, None),
        P("col", "row", None),
        P(),
        P(),
        P(),
    )
    out_specs = (P("row", "col", None, None), P("col", "row", None))
    body = functools.partial(shards, mesh.shape["row"], mesh.shape["col"])
    return jax.shard_map(body, mesh=mesh, in_specs=in_specs, out_specs=out_specs, check_vma=False)
```

profile of v0, /device:TPU:16, one launch (start us, length us, event | category | flops | bytes accessed | tf_op | source)
XLA Modules:
  0.0 81.7 jit_solution(6689011938831701834)
XLA Ops:
  0.6 77.3 %shard_map.86 = (bf16[1024,512]{1,0:T(8,128)(2,1)}, bf16[64,512]{1,0:T(8,128)(2,1)}) custom-call(bf16[1024,512]{1,0:T(8,128)(2,1)} %bitcast.8, s32[1,1024]{1,0:T(1,128)} %bitcast.10, s32[8,128]{1,0:T(8,128)} %bitcast.11, bf16[64,512]{1,0:T(8,128)(2,1)} %bitcast.9, bf16[2,1536,512]{2,1,0:T(8,128)(2,1)} %w_in_hbm.1, bf16[2,2,2,512,512]{4,3,2,1,0:T(8,128)(2,1)} %w_res_hbm.1, ...), custom_call_target="tpu_custom_call" | custom-call | flops 11000000512 | bytes 12000000 | tf_op jit(solution)/shard_map/pallas_call | solution.py:263
  78.0 2.3 %copy.11 = bf16[1,1,1024,512]{3,2,1,0:T(8,128)(2,1)} copy(bf16[1,1,1024,512]{3,2,1,0:T(8,128)(2,1)} %bitcast.6) | data formatting | bytes 2097152
  80.2 1.5 %copy.12 = bf16[1,64,512]{2,1,0:T(8,128)(2,1)} copy(bf16[1,64,512]{2,1,0:T(8,128)(2,1)} %bitcast.7) | data formatting | bytes 131072
where the time goes:
time: 81.9 us; the launch traced here: 81.7 us
  Pallas kernels  77.3 us (94%)
  local copies, waits for them, and re-layouts  3.73 us (5%)
    pallas_call x1, Pallas kernels, shards(): pl.pallas_call(functools.partial(kernel, rows_n, cols_n), out_shape=(jax....  77.3 us
    unnamed x2, local copies, waits for them, and re-layouts  3.73 us

commit v1 on v0

--- a/solution.py
+++ b/solution.py
@@ -10,6 +10,8 @@
 
 OFFSETS = (0, 0, 1, -1, 2, -2, 3, -3)
 ROOT_HALF = 0.7071067811865476
+PIECES = 4
+ORDER = (0, 3, 2, 1)
 MESH = pl.DeviceIdType.MESH
 F32 = jnp.float32
 BF16 = jnp.bfloat16
@@ -40,13 +42,14 @@
     w_res,
     w_node,
     cur,
+    hot_part,
+    acc,
     onehot,
     perm,
     base,
-    own_part,
-    h_tgt,
     pre,
     h_own,
+    h_tgt,
     h_all,
     part_out,
     part_in,
@@ -65,19 +68,31 @@
     edges, feat = msg.shape
     share = node.shape[0]
     points = share * rows_n
-    block = edges // len(OFFSETS)
+    blocks = len(OFFSETS)
+    block = edges // blocks
     pair = 2 * block
+    pairs = edges // pair
+    half = points // 2
     agg_scale = 1.0 / math.sqrt(edges // share)
     layers = w_in_hbm.shape[0]
-
-    def row_peer(j):
-        return lax.rem(r + j, rows_n)
+    along_x = rows_n // 2
+    r_y, r_x = r // along_x, lax.rem(r, along_x)
+    steps = [(dx, dy) for dy in (1, 0) for dx in (2, 1, 3, 0)]
+    others = rows_n - 1
+
+    def row_peer(j, sign=1):
+        dx, dy = steps[j]
+        x = lax.rem(r_x + along_x + sign * dx, along_x)
+        return lax.rem(r_y + dy, 2) * along_x + x
 
     def col_peer(offset):
         return lax.rem(c + offset + cols_n, cols_n)
 
+    def rows_of(device):
+        return pl.ds(pl.multiple_of(device * share, share), share)
+
     barrier = pltpu.get_barrier_semaphore()
-    for j in range(1, rows_n):
+    for j in range(others):
         pl.semaphore_signal(barrier, inc=1, device_id=(row_peer(j), c), device_id_type=MESH)
     for off in OFFSETS[2:]:
         pl.semaphore_signal(barrier, inc=1, device_id=(r, col_peer(off)), device_id_type=MESH)
@@ -92,32 +107,32 @@
 
     def rs_copy(t, j):
         return pltpu.make_async_remote_copy(
-            src_ref=part_out.at[t, j - 1],
-            dst_ref=part_in.at[t, j - 1],
-            send_sem=rs_send.at[t, j - 1],
-            recv_sem=rs_recv.at[t, j - 1],
+            src_ref=part_out.at[t, j],
+            dst_ref=part_in.at[t, j],
+            send_sem=rs_send.at[t, j],
+            recv_sem=rs_recv.at[t, j],
             device_id=(row_peer(j), c),
             device_id_type=MESH,
         )
 
     def ag_copy(t, j):
-        mine = pl.ds(pl.multiple_of(r * share, share), share)
-        return pltpu.make_async_remote_copy(
-            src_ref=h_all.at[t, mine],
-            dst_ref=h_all.at[t, mine],
-            send_sem=ag_send.at[t, j - 1],
-            recv_sem=ag_recv.at[t, j - 1],
+        target = h_all.at[t, rows_of(r)]
+        return pltpu.make_async_remote_copy(
+            src_ref=target,
+            dst_ref=target,
+            send_sem=ag_send.at[t, j],
+            recv_sem=ag_recv.at[t, j],
             device_id=(row_peer(j), c),
             device_id_type=MESH,
         )
 
     def ag_arrival(t, j):
-        theirs = pl.ds(pl.multiple_of(row_peer(rows_n - j) * share, share), share)
-        return pltpu.make_async_remote_copy(
-            src_ref=h_all.at[t, theirs],
-            dst_ref=h_all.at[t, theirs],
-            send_sem=ag_send.at[t, j - 1],
-            recv_sem=ag_recv.at[t, j - 1],
+        target = h_all.at[t, rows_of(row_peer(j, -1))]
+        return pltpu.make_async_remote_copy(
+            src_ref=target,
+            dst_ref=target,
+            send_sem=ag_send.at[t, j],
+            recv_sem=ag_recv.at[t, j],
             device_id=(row_peer(j), c),
             device_id_type=MESH,
         )
@@ -142,29 +157,31 @@
             device_id_type=MESH,
         )
 
-    def send_parts(t, messages):
-        half = points // 2
-        per = rows_n // 2
-        for part in range(2):
-            first = lax.rem(r + 1 + part * per, rows_n) * share
-            ids = lax.rem(lax.broadcasted_iota(jnp.int32, (half, edges), 0) + first, points)
-            hot = jnp.where(tgt[...] == ids, 1.0, 0.0).astype(BF16)
-            sums = mm(hot, messages[...])
-            for i in range(per):
-                j = part * per + i + 1
-                rows = sums[i * share : (i + 1) * share]
-                if j == rows_n:
-                    own_part[...] = rows
-                    continue
-                part_out[t, j - 1] = rows.astype(BF16)
-                if t == 0 and j == 1:
-                    pl.semaphore_wait(barrier, rows_n - 1 + len(OFFSETS) - 2)
-                rs_copy(t, j).start()
-
-    send_parts(0, msg)
+    def send_sums(t, part, sums):
+        for i in range(rows_n // 2):
+            j = part * (rows_n // 2) + i
+            if j == others:
+                continue
+            part_out[t, j] = sums[i * share : (i + 1) * share].astype(BF16)
+            if t == 0 and j == 0:
+                pl.semaphore_wait(barrier, others + blocks - 2)
+            rs_copy(t, j).start()
+
+    for part in range(2):
+        for i in range(rows_n // 2):
+            j = part * (rows_n // 2) + i
+            ids = lax.broadcasted_iota(jnp.int32, (share, edges), 0) + row_peer(j) * share
+            hot_part[j * share : (j + 1) * share] = jnp.where(
+                tgt[...] == ids, 1.0, 0.0
+            ).astype(BF16)
+        rows = pl.ds(part * half, half)
+        sums = mm(hot_part[rows], msg[...])
+        send_sums(0, part, sums)
+        if part:
+            acc[rows] = sums
 
     lane = lax.broadcasted_iota(jnp.int32, (block, block), 1)
-    for k in range(len(OFFSETS)):
+    for k in range(blocks):
         rows = pl.ds(k * block, block)
         ids = jnp.broadcast_to(tgt[0:1, k * block : (k + 1) * block], (block, block)).T
         for i in range(points // block):
@@ -179,25 +196,25 @@
         last = t == layers - 1
         held = msg if t == 0 else cur
         loads[3 * t].wait()
-        for q in range(edges // pair):
+        for q in range(pairs):
             rows = pl.ds(q * pair, pair)
             base[rows] = mm(held[rows], w_in[t, :feat])
 
         loads[3 * t + 1].wait()
-        total = own_part[...]
-        for j in range(1, rows_n):
+        total = acc[others * share :]
+        for j in range(others):
             rs_copy(t, j).wait_recv()
-            total = total + part_in[t, j - 1].astype(F32)
+            total = total + part_in[t, j].astype(F32)
         scaled = (total * agg_scale).astype(BF16)
         h_new = (h_own[...].astype(F32) + silu(mm(scaled, w_node[t]))).astype(BF16)
         h_own[...] = h_new
-        h_all[t, pl.ds(pl.multiple_of(r * share, share), share)] = h_new
-        for j in range(1, rows_n):
+        h_all[t, rows_of(r)] = h_new
+        for j in range(others):
             ag_copy(t, j).start()
         if last:
-            node_copy = pltpu.make_async_copy(h_own, node_out, out_sem.at[edges // pair])
+            node_copy = pltpu.make_async_copy(h_own, node_out, out_sem.at[pairs])
             node_copy.start()
-        for j in range(1, rows_n):
+        for j in range(others):
             ag_arrival(t, j).wait_recv()
 
         for q in (3, 2, 1, 0):
@@ -210,12 +227,12 @@
                 u_out[t, b] = u[i * block : (i + 1) * block]
                 if q:
                     col_copy(t, b).start()
-        for q in (0, 1, 2, 3):
+        for q in ORDER:
             rows = pl.ds(q * pair, pair)
             pre[rows] = mm(h_tgt[rows], w_in[t, 2 * feat :])
 
         loads[3 * t + 2].wait()
-        for q in (0, 1, 2, 3):
+        for q in ORDER:
             rows = pl.ds(q * pair, pair)
             moved = []
             for k in (2 * q, 2 * q + 1):
@@ -231,22 +248,49 @@
             ).astype(BF16)
             inner = silu(mm(hidden, w_res[t, 1, 0])).astype(BF16)
             summed = (hidden.astype(F32) + silu(mm(inner, w_res[t, 1, 1]))) * ROOT_HALF
-            cur[rows] = ((held[rows].astype(F32) + summed) * ROOT_HALF).astype(BF16)
+            new = ((held[rows].astype(F32) + summed) * ROOT_HALF).astype(BF16)
+            cur[rows] = new
             if last:
                 pltpu.make_async_copy(cur.at[rows], edge_out.at[rows], out_sem.at[q]).start()
-        if not last:
-            send_parts(t + 1, cur)
+                continue
+            columns = slice(q * pair, (q + 1) * pair)
+            for part in range(2):
+                points_of = pl.ds(part * half, half)
+                sums = mm(hot_part[points_of, columns], new)
+                if q:
+                    sums = acc[points_of] + sums
+                if q == ORDER[-1]:
+                    send_sums(t + 1, part, sums)
+                if q != ORDER[-1] or part:
+                    acc[points_of] = sums
 
     for t in range(layers):
-        for j in range(1, rows_n):
+        for j in range(others):
             rs_copy(t, j).wait_send()
             ag_copy(t, j).wait_send()
-        for b in range(2, len(OFFSETS)):
+        for b in range(2, blocks):
             col_copy(t, b).wait_send()
-    for q in range(edges // pair):
+    for q in range(pairs):
         rows = pl.ds(q * pair, pair)
         pltpu.make_async_copy(cur.at[rows], edge_out.at[rows], out_sem.at[q]).wait()
     node_copy.wait()
+
+
+def hand_over(edge_in, node_in, edge_out, node_out, edge_held, node_held, sems):
+    piece = edge_in.shape[0] // PIECES
+    moves = [(node_in, node_held, node_out)]
+    for i in range(PIECES):
+        rows = pl.ds(i * piece, piece)
+        moves.append((edge_in.at[rows], edge_held.at[rows], edge_out.at[rows]))
+    loads = [pltpu.make_async_copy(m[0], m[1], sems.at[0, i]) for i, m in enumerate(moves)]
+    stores = [pltpu.make_async_copy(m[1], m[2], sems.at[1, i]) for i, m in enumerate(moves)]
+    for copy in loads:
+        copy.start()
+    for load, store in zip(loads, stores):
+        load.wait()
+        store.start()
+    for copy in stores:
+        copy.wait()
 
 
 def shards(rows_n, cols_n, messages, targets, reverse_rows, nodes, w_in, w_res, w_node):
@@ -260,12 +304,13 @@
     dma = pltpu.SemaphoreType.DMA
     vmem = pl.BlockSpec(memory_space=pltpu.VMEM)
     hbm = pl.BlockSpec(memory_space=pl.ANY)
-    edge_out, node_out = pl.pallas_call(
+    shapes = (
+        jax.ShapeDtypeStruct((edges, feat), BF16),
+        jax.ShapeDtypeStruct((share, feat), BF16),
+    )
+    held = pl.pallas_call(
         functools.partial(kernel, rows_n, cols_n),
-        out_shape=(
-            jax.ShapeDtypeStruct((edges, feat), BF16),
-            jax.ShapeDtypeStruct((share, feat), BF16),
-        ),
+        out_shape=shapes,
         in_specs=[vmem] * 4 + [hbm] * 3,
         out_specs=(hbm, hbm),
         scratch_shapes=[
@@ -273,13 +318,14 @@
             pltpu.VMEM(w_res.shape, BF16),
             pltpu.VMEM(w_node.shape, BF16),
             pltpu.VMEM((edges, feat), BF16),
+            pltpu.VMEM((points, edges), BF16),
+            pltpu.VMEM((points, feat), F32),
             pltpu.VMEM((edges, points), BF16),
             pltpu.VMEM((blocks, block, block), BF16),
             pltpu.VMEM((edges, feat), F32),
-            pltpu.VMEM((share, feat), F32),
-            pltpu.VMEM((edges, feat), BF16),
             pltpu.VMEM((edges, feat), F32),
             pltpu.VMEM((share, feat), BF16),
+            pltpu.VMEM((edges, feat), BF16),
             pltpu.VMEM((layers, points, feat), BF16),
             pltpu.VMEM((layers, rows_n - 1, share, feat), BF16),
             pltpu.VMEM((layers, rows_n - 1, share, feat), BF16),
@@ -301,6 +347,13 @@
             flops=11 * 10**9, bytes_accessed=12 * 10**6, transcendentals=5 * 10**6
         ),
     )(msg, tgt, rev, node, w_in, w_res, w_node)
+    edge_out, node_out = pl.pallas_call(
+        hand_over,
+        out_shape=shapes,
+        in_specs=[hbm] * 2,
+        out_specs=(hbm, hbm),
+        scratch_shapes=[pltpu.VMEM((edges, feat), BF16), pltpu.VMEM((share, feat), BF16), dma((2, PIECES + 1))],
+    )(*held)
     return edge_out[None, None], node_out[None]
 
 

time: 81.9 us -> 74.3 us (0.907)
  the two profiles are of different devices: /device:TPU:16 before, /device:TPU:1 now
where the time goes in v1:
time: 74.3 us; the launch traced here: 74.1 us
  Pallas kernels  73.5 us (99%)
    pallas_call x1, Pallas kernels, shards(): pl.pallas_call(functools.partial(kernel, rows_n, cols_n), out_shape=shape...  71.5 us
    pallas_call x1, Pallas kernels, shards(): pl.pallas_call(hand_over, out_shape=shapes, in_specs=[hbm] * 2, out_specs...  2.04 us

profile of v1, /device:TPU:1, one launch (start us, length us, event | category | flops | bytes accessed | tf_op | source)
XLA Modules:
  0.0 74.1 jit_solution(1394915911946294533)
XLA Ops:
  0.6 71.5 %shard_map.86 = (bf16[1024,512]{1,0:T(8,128)(2,1)}, bf16[64,512]{1,0:T(8,128)(2,1)}) custom-call(bf16[1024,512]{1,0:T(8,128)(2,1)} %bitcast.6, s32[1,1024]{1,0:T(1,128)} %bitcast.10, s32[8,128]{1,0:T(8,128)} %bitcast.11, bf16[64,512]{1,0:T(8,128)(2,1)} %bitcast.8, bf16[2,1536,512]{2,1,0:T(8,128)(2,1)} %w_in_hbm.1, bf16[2,2,2,512,512]{4,3,2,1,0:T(8,128)(2,1)} %w_res_hbm.1, ...), custom_call_target="tpu_custom_call" | custom-call | flops 11000000512 | bytes 12000000 | tf_op jit(solution)/shard_map/pallas_call | solution.py:311
  72.1 2.0 %shard_map.87 = (bf16[1024,512]{1,0:T(8,128)(2,1)}, bf16[64,512]{1,0:T(8,128)(2,1)}) custom-call(bf16[1024,512]{1,0:T(8,128)(2,1)} %get-tuple-element.6.edge_in, bf16[64,512]{1,0:T(8,128)(2,1)} %get-tuple-element.7.node_in), custom_call_target="tpu_custom_call" | custom-call | tf_op jit(solution)/shard_map/pallas_call | solution.py:350

commit v2 on v1

--- a/solution.py
+++ b/solution.py
@@ -10,6 +10,7 @@
 
 OFFSETS = (0, 0, 1, -1, 2, -2, 3, -3)
 ROOT_HALF = 0.7071067811865476
+PARTS = 2
 PIECES = 4
 ORDER = (0, 3, 2, 1)
 MESH = pl.DeviceIdType.MESH
@@ -29,10 +30,10 @@
 def kernel(
     rows_n,
     cols_n,
-    msg,
-    tgt,
-    rev,
-    node,
+    msg_hbm,
+    tgt_hbm,
+    rev_hbm,
+    node_hbm,
     w_in_hbm,
     w_res_hbm,
     w_node_hbm,
@@ -41,6 +42,9 @@
     w_in,
     w_res,
     w_node,
+    tgt,
+    rev,
+    msg,
     cur,
     hot_part,
     acc,
@@ -62,17 +66,19 @@
     ag_recv,
     col_send,
     col_recv,
+    in_sem,
     out_sem,
 ):
     r, c = lax.axis_index("row"), lax.axis_index("col")
-    edges, feat = msg.shape
-    share = node.shape[0]
+    edges, feat = msg_hbm.shape
+    share = node_hbm.shape[0]
     points = share * rows_n
     blocks = len(OFFSETS)
     block = edges // blocks
     pair = 2 * block
     pairs = edges // pair
-    half = points // 2
+    group = points // PARTS
+    piece = share // PARTS
     agg_scale = 1.0 / math.sqrt(edges // share)
     layers = w_in_hbm.shape[0]
     along_x = rows_n // 2
@@ -88,8 +94,8 @@
     def col_peer(offset):
         return lax.rem(c + offset + cols_n, cols_n)
 
-    def rows_of(device):
-        return pl.ds(pl.multiple_of(device * share, share), share)
+    def rows_of(device, part):
+        return pl.ds(pl.multiple_of(device * share + part * piece, piece), piece)
 
     barrier = pltpu.get_barrier_semaphore()
     for j in range(others):
@@ -97,6 +103,12 @@
     for off in OFFSETS[2:]:
         pl.semaphore_signal(barrier, inc=1, device_id=(r, col_peer(off)), device_id_type=MESH)
 
+    firsts = []
+    for i, (src, dst) in enumerate(
+        ((tgt_hbm, tgt), (msg_hbm, msg), (rev_hbm, rev), (node_hbm, h_own))
+    ):
+        firsts.append(pltpu.make_async_copy(src, dst, in_sem.at[i]))
+        firsts[-1].start()
     loads = []
     for t in range(layers):
         for i, (src, dst) in enumerate(
@@ -105,34 +117,34 @@
             loads.append(pltpu.make_async_copy(src.at[t], dst.at[t], w_sem.at[t, i]))
             loads[-1].start()
 
-    def rs_copy(t, j):
-        return pltpu.make_async_remote_copy(
-            src_ref=part_out.at[t, j],
-            dst_ref=part_in.at[t, j],
-            send_sem=rs_send.at[t, j],
-            recv_sem=rs_recv.at[t, j],
+    def rs_copy(t, part, j):
+        return pltpu.make_async_remote_copy(
+            src_ref=part_out.at[t, part, j],
+            dst_ref=part_in.at[t, part, j],
+            send_sem=rs_send.at[t, part, j],
+            recv_sem=rs_recv.at[t, part, j],
             device_id=(row_peer(j), c),
             device_id_type=MESH,
         )
 
-    def ag_copy(t, j):
-        target = h_all.at[t, rows_of(r)]
+    def ag_copy(t, part, j):
+        target = h_all.at[t, rows_of(r, part)]
         return pltpu.make_async_remote_copy(
             src_ref=target,
             dst_ref=target,
-            send_sem=ag_send.at[t, j],
-            recv_sem=ag_recv.at[t, j],
+            send_sem=ag_send.at[t, part, j],
+            recv_sem=ag_recv.at[t, part, j],
             device_id=(row_peer(j), c),
             device_id_type=MESH,
         )
 
-    def ag_arrival(t, j):
-        target = h_all.at[t, rows_of(row_peer(j, -1))]
+    def ag_arrival(t, part, j):
+        target = h_all.at[t, rows_of(row_peer(j, -1), part)]
         return pltpu.make_async_remote_copy(
             src_ref=target,
             dst_ref=target,
-            send_sem=ag_send.at[t, j],
-            recv_sem=ag_recv.at[t, j],
+            send_sem=ag_send.at[t, part, j],
+            recv_sem=ag_recv.at[t, part, j],
             device_id=(row_peer(j), c),
             device_id_type=MESH,
         )
@@ -158,28 +170,26 @@
         )
 
     def send_sums(t, part, sums):
-        for i in range(rows_n // 2):
-            j = part * (rows_n // 2) + i
-            if j == others:
-                continue
-            part_out[t, j] = sums[i * share : (i + 1) * share].astype(BF16)
-            if t == 0 and j == 0:
+        for j in range(others):
+            part_out[t, part, j] = sums[j * piece : (j + 1) * piece].astype(BF16)
+            if t == 0 and part == 0 and j == 0:
                 pl.semaphore_wait(barrier, others + blocks - 2)
-            rs_copy(t, j).start()
-
-    for part in range(2):
-        for i in range(rows_n // 2):
-            j = part * (rows_n // 2) + i
-            ids = lax.broadcasted_iota(jnp.int32, (share, edges), 0) + row_peer(j) * share
-            hot_part[j * share : (j + 1) * share] = jnp.where(
-                tgt[...] == ids, 1.0, 0.0
-            ).astype(BF16)
-        rows = pl.ds(part * half, half)
-        sums = mm(hot_part[rows], msg[...])
-        send_sums(0, part, sums)
-        if part:
-            acc[rows] = sums
-
+            rs_copy(t, part, j).start()
+        acc[part * group + others * piece : (part + 1) * group] = sums[others * piece :]
+
+    firsts[0].wait()
+    for part in range(PARTS):
+        for j in range(rows_n):
+            ids = lax.broadcasted_iota(jnp.int32, (piece, edges), 0) + (
+                row_peer(j) * share + part * piece
+            )
+            first = part * group + j * piece
+            hot_part[first : first + piece] = jnp.where(tgt[...] == ids, 1.0, 0.0).astype(BF16)
+        if part == 0:
+            firsts[1].wait()
+        send_sums(0, part, mm(hot_part[part * group : (part + 1) * group], msg[...]))
+
+    firsts[2].wait()
     lane = lax.broadcasted_iota(jnp.int32, (block, block), 1)
     for k in range(blocks):
         rows = pl.ds(k * block, block)
@@ -191,7 +201,8 @@
         ids = jnp.broadcast_to(rev[k : k + 1, :], (block, block)).T
         perm[k] = jnp.where(ids == lane, 1.0, 0.0).astype(BF16)
 
-    h_own[...] = node[...]
+    firsts[3].wait()
+    edge_copies = []
     for t in range(layers):
         last = t == layers - 1
         held = msg if t == 0 else cur
@@ -201,21 +212,24 @@
             base[rows] = mm(held[rows], w_in[t, :feat])
 
         loads[3 * t + 1].wait()
-        total = acc[others * share :]
-        for j in range(others):
-            rs_copy(t, j).wait_recv()
-            total = total + part_in[t, j].astype(F32)
-        scaled = (total * agg_scale).astype(BF16)
-        h_new = (h_own[...].astype(F32) + silu(mm(scaled, w_node[t]))).astype(BF16)
-        h_own[...] = h_new
-        h_all[t, rows_of(r)] = h_new
-        for j in range(others):
-            ag_copy(t, j).start()
+        for part in range(PARTS):
+            total = acc[part * group + others * piece : (part + 1) * group]
+            for j in range(others):
+                rs_copy(t, part, j).wait_recv()
+                total = total + part_in[t, part, j].astype(F32)
+            scaled = (total * agg_scale).astype(BF16)
+            mine = slice(part * piece, (part + 1) * piece)
+            h_new = (h_own[mine].astype(F32) + silu(mm(scaled, w_node[t]))).astype(BF16)
+            h_own[mine] = h_new
+            h_all[t, rows_of(r, part)] = h_new
+            for j in range(others):
+                ag_copy(t, part, j).start()
         if last:
             node_copy = pltpu.make_async_copy(h_own, node_out, out_sem.at[pairs])
             node_copy.start()
-        for j in range(others):
-            ag_arrival(t, j).wait_recv()
+        for part in range(PARTS):
+            for j in range(others):
+                ag_arrival(t, part, j).wait_recv()
 
         for q in (3, 2, 1, 0):
             rows = pl.ds(q * pair, pair)
@@ -251,28 +265,29 @@
             new = ((held[rows].astype(F32) + summed) * ROOT_HALF).astype(BF16)
             cur[rows] = new
             if last:
-                pltpu.make_async_copy(cur.at[rows], edge_out.at[rows], out_sem.at[q]).start()
+                edge_copies.append(pltpu.make_async_copy(cur.at[rows], edge_out.at[rows], out_sem.at[q]))
+                edge_copies[-1].start()
                 continue
             columns = slice(q * pair, (q + 1) * pair)
-            for part in range(2):
-                points_of = pl.ds(part * half, half)
+            for part in range(PARTS):
+                points_of = pl.ds(part * group, group)
                 sums = mm(hot_part[points_of, columns], new)
-                if q:
+                if q != ORDER[0]:
                     sums = acc[points_of] + sums
                 if q == ORDER[-1]:
                     send_sums(t + 1, part, sums)
-                if q != ORDER[-1] or part:
+                else:
                     acc[points_of] = sums
 
     for t in range(layers):
-        for j in range(others):
-            rs_copy(t, j).wait_send()
-            ag_copy(t, j).wait_send()
+        for part in range(PARTS):
+            for j in range(others):
+                rs_copy(t, part, j).wait_send()
+                ag_copy(t, part, j).wait_send()
         for b in range(2, blocks):
             col_copy(t, b).wait_send()
-    for q in range(pairs):
-        rows = pl.ds(q * pair, pair)
-        pltpu.make_async_copy(cur.at[rows], edge_out.at[rows], out_sem.at[q]).wait()
+    for copy in edge_copies:
+        copy.wait()
     node_copy.wait()
 
 
@@ -302,8 +317,7 @@
     blocks = len(OFFSETS)
     block = edges // blocks
     dma = pltpu.SemaphoreType.DMA
-    vmem = pl.BlockSpec(memory_space=pltpu.VMEM)
-    hbm = pl.BlockSpec(memory_space=pl.ANY)
+    hbm = pl.BlockSpec(memory_space=pltpu.HBM)
     shapes = (
         jax.ShapeDtypeStruct((edges, feat), BF16),
         jax.ShapeDtypeStruct((share, feat), BF16),
@@ -311,12 +325,15 @@
     held = pl.pallas_call(
         functools.partial(kernel, rows_n, cols_n),
         out_shape=shapes,
-        in_specs=[vmem] * 4 + [hbm] * 3,
+        in_specs=[hbm] * 7,
         out_specs=(hbm, hbm),
         scratch_shapes=[
             pltpu.VMEM(w_in.shape, BF16),
             pltpu.VMEM(w_res.shape, BF16),
             pltpu.VMEM(w_node.shape, BF16),
+            pltpu.VMEM(tgt.shape, tgt.dtype),
+            pltpu.VMEM(rev.shape, rev.dtype),
+            pltpu.VMEM((edges, feat), BF16),
             pltpu.VMEM((edges, feat), BF16),
             pltpu.VMEM((points, edges), BF16),
             pltpu.VMEM((points, feat), F32),
@@ -327,17 +344,18 @@
             pltpu.VMEM((share, feat), BF16),
             pltpu.VMEM((edges, feat), BF16),
             pltpu.VMEM((layers, points, feat), BF16),
-            pltpu.VMEM((layers, rows_n - 1, share, feat), BF16),
-            pltpu.VMEM((layers, rows_n - 1, share, feat), BF16),
+            pltpu.VMEM((layers, PARTS, rows_n - 1, share // PARTS, feat), BF16),
+            pltpu.VMEM((layers, PARTS, rows_n - 1, share // PARTS, feat), BF16),
             pltpu.VMEM((layers, blocks, block, feat), BF16),
             pltpu.VMEM((layers, blocks - 2, block, feat), BF16),
             dma((layers, 3)),
-            dma((layers, rows_n - 1)),
-            dma((layers, rows_n - 1)),
-            dma((layers, rows_n - 1)),
-            dma((layers, rows_n - 1)),
+            dma((layers, PARTS, rows_n - 1)),
+            dma((layers, PARTS, rows_n - 1)),
+            dma((layers, PARTS, rows_n - 1)),
+            dma((layers, PARTS, rows_n - 1)),
             dma((layers, blocks - 2)),
             dma((layers, blocks - 2)),
+            dma((4,)),
             dma((blocks // 2 + 1,)),
         ],
         compiler_params=pltpu.CompilerParams(

time: 74.3 us -> 69.7 us (0.938)
  Pallas kernels: 73.5 us -> 69 us
    pallas_call x1, Pallas kernels: 71.5 us -> 66.9 us  [shards(): pl.pallas_call(functools.partial(kernel, rows_n, cols_n), out_shape=shape...]
where the time goes in v2:
time: 69.7 us; the launch traced here: 69.6 us
  Pallas kernels  69 us (99%)
    pallas_call x1, Pallas kernels, shards(): pl.pallas_call(functools.partial(kernel, rows_n, cols_n), out_shape=shape...  66.9 us
    pallas_call x1, Pallas kernels, shards(): pl.pallas_call(hand_over, out_shape=shapes, in_specs=[hbm] * 2, out_specs...  2.04 us

profile of v2, /device:TPU:1, one launch (start us, length us, event | category | flops | bytes accessed | tf_op | source)
XLA Modules:
  0.0 69.6 jit_solution(8006312196030388634)
XLA Ops:
  0.6 66.9 %shard_map.86 = (bf16[1024,512]{1,0:T(8,128)(2,1)}, bf16[64,512]{1,0:T(8,128)(2,1)}) custom-call(bf16[1024,512]{1,0:T(8,128)(2,1)} %bitcast.6, s32[1,1024]{1,0:T(1,128)} %bitcast.10, s32[8,128]{1,0:T(8,128)} %bitcast.11, bf16[64,512]{1,0:T(8,128)(2,1)} %bitcast.8, bf16[2,1536,512]{2,1,0:T(8,128)(2,1)} %w_in_hbm.1, bf16[2,2,2,512,512]{4,3,2,1,0:T(8,128)(2,1)} %w_res_hbm.1, ...), custom_call_target="tpu_custom_call" | custom-call | flops 11000000512 | bytes 12000000 | tf_op jit(solution)/shard_map/pallas_call | solution.py:325
  67.6 2.0 %shard_map.87 = (bf16[1024,512]{1,0:T(8,128)(2,1)}, bf16[64,512]{1,0:T(8,128)(2,1)}) custom-call(bf16[1024,512]{1,0:T(8,128)(2,1)} %get-tuple-element.6.edge_in, bf16[64,512]{1,0:T(8,128)(2,1)} %get-tuple-element.7.node_in), custom_call_target="tpu_custom_call" | custom-call | tf_op jit(solution)/shard_map/pallas_call | solution.py:368

commit v3 on v2

--- a/solution.py
+++ b/solution.py
@@ -49,11 +49,12 @@
     hot_part,
     acc,
     onehot,
+    onehot_sent,
     perm,
+    m_sent,
     base,
     pre,
     h_own,
-    h_tgt,
     h_all,
     part_out,
     part_in,
@@ -109,20 +110,12 @@
     ):
         firsts.append(pltpu.make_async_copy(src, dst, in_sem.at[i]))
         firsts[-1].start()
-    loads = []
-    for t in range(layers):
-        for i, (src, dst) in enumerate(
-            ((w_in_hbm, w_in), (w_node_hbm, w_node), (w_res_hbm, w_res))
-        ):
-            loads.append(pltpu.make_async_copy(src.at[t], dst.at[t], w_sem.at[t, i]))
-            loads[-1].start()
-
     def rs_copy(t, part, j):
         return pltpu.make_async_remote_copy(
             src_ref=part_out.at[t, part, j],
             dst_ref=part_in.at[t, part, j],
-            send_sem=rs_send.at[t, part, j],
-            recv_sem=rs_recv.at[t, part, j],
+            send_sem=rs_send.at[t, part],
+            recv_sem=rs_recv.at[t, part],
             device_id=(row_peer(j), c),
             device_id_type=MESH,
         )
@@ -132,22 +125,35 @@
         return pltpu.make_async_remote_copy(
             src_ref=target,
             dst_ref=target,
-            send_sem=ag_send.at[t, part, j],
-            recv_sem=ag_recv.at[t, part, j],
+            send_sem=ag_send.at[t, part],
+            recv_sem=ag_recv.at[t, part],
             device_id=(row_peer(j), c),
             device_id_type=MESH,
         )
 
-    def ag_arrival(t, part, j):
-        target = h_all.at[t, rows_of(row_peer(j, -1), part)]
-        return pltpu.make_async_remote_copy(
-            src_ref=target,
-            dst_ref=target,
-            send_sem=ag_send.at[t, part, j],
-            recv_sem=ag_recv.at[t, part, j],
-            device_id=(row_peer(j), c),
-            device_id_type=MESH,
-        )
+    def rs_all(t, part):
+        return pltpu.make_async_remote_copy(
+            src_ref=part_out.at[t, part],
+            dst_ref=part_in.at[t, part],
+            send_sem=rs_send.at[t, part],
+            recv_sem=rs_recv.at[t, part],
+            device_id=(row_peer(0), c),
+            device_id_type=MESH,
+        )
+
+    def ag_all(t, part):
+        rows = h_all.at[t, pl.ds(0, others * piece)]
+        return pltpu.make_async_remote_copy(
+            src_ref=rows,
+            dst_ref=rows,
+            send_sem=ag_send.at[t, part],
+            recv_sem=ag_recv.at[t, part],
+            device_id=(row_peer(0), c),
+            device_id_type=MESH,
+        )
+
+    def blocks_of(q):
+        return (2 * q, 2 * q + 1) if q else ()
 
     def col_copy(t, b):
         return pltpu.make_async_remote_copy(
@@ -189,8 +195,17 @@
             firsts[1].wait()
         send_sums(0, part, mm(hot_part[part * group : (part + 1) * group], msg[...]))
 
+    loads = []
+    for t in range(layers):
+        for i, (src, dst) in enumerate(
+            ((w_in_hbm, w_in), (w_node_hbm, w_node), (w_res_hbm, w_res))
+        ):
+            loads.append(pltpu.make_async_copy(src.at[t], dst.at[t], w_sem.at[t, i]))
+            loads[-1].start()
+
     firsts[2].wait()
     lane = lax.broadcasted_iota(jnp.int32, (block, block), 1)
+    sublane = lax.broadcasted_iota(jnp.int32, (block, block), 0)
     for k in range(blocks):
         rows = pl.ds(k * block, block)
         ids = jnp.broadcast_to(tgt[0:1, k * block : (k + 1) * block], (block, block)).T
@@ -198,8 +213,9 @@
             onehot[rows, i * block : (i + 1) * block] = jnp.where(
                 ids == lane + i * block, 1.0, 0.0
             ).astype(BF16)
-        ids = jnp.broadcast_to(rev[k : k + 1, :], (block, block)).T
-        perm[k] = jnp.where(ids == lane, 1.0, 0.0).astype(BF16)
+        ids = jnp.broadcast_to(rev[k : k + 1, :], (block, block))
+        perm[k] = jnp.where(ids == sublane, 1.0, 0.0).astype(BF16)
+        onehot_sent[rows] = mm(perm[k], onehot[rows]).astype(BF16)
 
     firsts[3].wait()
     edge_copies = []
@@ -207,15 +223,18 @@
         last = t == layers - 1
         held = msg if t == 0 else cur
         loads[3 * t].wait()
+        for k in range(blocks):
+            rows = pl.ds(k * block, block)
+            m_sent[rows] = mm(perm[k], held[rows]).astype(BF16)
         for q in range(pairs):
             rows = pl.ds(q * pair, pair)
-            base[rows] = mm(held[rows], w_in[t, :feat])
+            base[rows] = mm(m_sent[rows], w_in[t, :feat])
 
         loads[3 * t + 1].wait()
         for part in range(PARTS):
             total = acc[part * group + others * piece : (part + 1) * group]
+            rs_all(t, part).wait_recv()
             for j in range(others):
-                rs_copy(t, part, j).wait_recv()
                 total = total + part_in[t, part, j].astype(F32)
             scaled = (total * agg_scale).astype(BF16)
             mine = slice(part * piece, (part + 1) * piece)
@@ -228,50 +247,63 @@
             node_copy = pltpu.make_async_copy(h_own, node_out, out_sem.at[pairs])
             node_copy.start()
         for part in range(PARTS):
-            for j in range(others):
-                ag_arrival(t, part, j).wait_recv()
+            ag_all(t, part).wait_recv()
 
         for q in (3, 2, 1, 0):
             rows = pl.ds(q * pair, pair)
-            picked = mm(onehot[rows], h_all[t]).astype(BF16)
-            h_tgt[rows] = picked
+            picked = mm(onehot_sent[rows], h_all[t]).astype(BF16)
             u = (base[rows] + mm(picked, w_in[t, feat : 2 * feat])).astype(BF16)
             for i in range(2):
-                b = 2 * q + i
-                u_out[t, b] = u[i * block : (i + 1) * block]
-                if q:
-                    col_copy(t, b).start()
+                u_out[t, 2 * q + i] = u[i * block : (i + 1) * block]
+            for b in blocks_of(q):
+                col_copy(t, b).start()
         for q in ORDER:
             rows = pl.ds(q * pair, pair)
-            pre[rows] = mm(h_tgt[rows], w_in[t, 2 * feat :])
+            picked = mm(onehot[rows], h_all[t]).astype(BF16)
+            pre[rows] = mm(picked, w_in[t, 2 * feat :])
 
         loads[3 * t + 2].wait()
-        for q in ORDER:
-            rows = pl.ds(q * pair, pair)
-            moved = []
-            for k in (2 * q, 2 * q + 1):
-                if q:
-                    col_arrival(t, k).wait_recv()
-                    moved.append(mm(perm[k], u_in[t, k - 2]))
-                else:
-                    moved.append(mm(perm[k], u_out[t, k ^ 1]))
-            hidden = silu(pre[rows] + jnp.concatenate(moved, axis=0)).astype(BF16)
+        def edge_layer(x1, m):
+            hidden = silu(x1).astype(BF16)
             inner = silu(mm(hidden, w_res[t, 0, 0])).astype(BF16)
             hidden = (
                 (hidden.astype(F32) + silu(mm(inner, w_res[t, 0, 1]))) * ROOT_HALF
             ).astype(BF16)
             inner = silu(mm(hidden, w_res[t, 1, 0])).astype(BF16)
             summed = (hidden.astype(F32) + silu(mm(inner, w_res[t, 1, 1]))) * ROOT_HALF
-            new = ((held[rows].astype(F32) + summed) * ROOT_HALF).astype(BF16)
-            cur[rows] = new
+            return ((m.astype(F32) + summed) * ROOT_HALF).astype(BF16)
+
+        for part in range(PARTS):
+            rs_all(t, part).wait_send()
+            ag_all(t, part).wait_send()
+        if t:
+            for b in blocks_of(ORDER[-1]):
+                col_copy(t - 1, b).wait_send()
+        for n, q in enumerate(ORDER):
+            if n > 1:
+                for b in blocks_of(ORDER[n - 1]):
+                    col_copy(t, b).wait_send()
+            rows = pl.ds(q * pair, pair)
+            arrived = []
+            for k in (2 * q, 2 * q + 1):
+                if q:
+                    col_arrival(t, k).wait_recv()
+                    arrived.append(u_in[t, k - 2])
+                else:
+                    arrived.append(u_out[t, k ^ 1])
+            sums = pre[rows] + jnp.concatenate(arrived, axis=0).astype(F32)
+            cur[rows] = edge_layer(sums, held[rows])
             if last:
-                edge_copies.append(pltpu.make_async_copy(cur.at[rows], edge_out.at[rows], out_sem.at[q]))
+                edge_copies.append(
+                    pltpu.make_async_copy(cur.at[rows], edge_out.at[rows], out_sem.at[q])
+                )
                 edge_copies[-1].start()
+            if last:
                 continue
             columns = slice(q * pair, (q + 1) * pair)
             for part in range(PARTS):
                 points_of = pl.ds(part * group, group)
-                sums = mm(hot_part[points_of, columns], new)
+                sums = mm(hot_part[points_of, columns], cur[rows])
                 if q != ORDER[0]:
                     sums = acc[points_of] + sums
                 if q == ORDER[-1]:
@@ -279,13 +311,8 @@
                 else:
                     acc[points_of] = sums
 
-    for t in range(layers):
-        for part in range(PARTS):
-            for j in range(others):
-                rs_copy(t, part, j).wait_send()
-                ag_copy(t, part, j).wait_send()
-        for b in range(2, blocks):
-            col_copy(t, b).wait_send()
+    for b in blocks_of(ORDER[-1]):
+        col_copy(layers - 1, b).wait_send()
     for copy in edge_copies:
         copy.wait()
     node_copy.wait()
@@ -338,21 +365,22 @@
             pltpu.VMEM((points, edges), BF16),
             pltpu.VMEM((points, feat), F32),
             pltpu.VMEM((edges, points), BF16),
+            pltpu.VMEM((edges, points), BF16),
             pltpu.VMEM((blocks, block, block), BF16),
+            pltpu.VMEM((edges, feat), BF16),
             pltpu.VMEM((edges, feat), F32),
             pltpu.VMEM((edges, feat), F32),
             pltpu.VMEM((share, feat), BF16),
-            pltpu.VMEM((edges, feat), BF16),
             pltpu.VMEM((layers, points, feat), BF16),
             pltpu.VMEM((layers, PARTS, rows_n - 1, share // PARTS, feat), BF16),
             pltpu.VMEM((layers, PARTS, rows_n - 1, share // PARTS, feat), BF16),
             pltpu.VMEM((layers, blocks, block, feat), BF16),
             pltpu.VMEM((layers, blocks - 2, block, feat), BF16),
             dma((layers, 3)),
-            dma((layers, PARTS, rows_n - 1)),
-            dma((layers, PARTS, rows_n - 1)),
-            dma((layers, PARTS, rows_n - 1)),
-            dma((layers, PARTS, rows_n - 1)),
+            dma((layers, PARTS)),
+            dma((layers, PARTS)),
+            dma((layers, PARTS)),
+            dma((layers, PARTS)),
             dma((layers, blocks - 2)),
             dma((layers, blocks - 2)),
             dma((4,)),

time: 69.7 us -> 68.2 us (0.978)
  Pallas kernels: 69 us -> 67.3 us
    pallas_call x1, Pallas kernels: 66.9 us -> 65.3 us  [shards(): pl.pallas_call(functools.partial(kernel, rows_n, cols_n), out_shape=shape...]
where the time goes in v3:
time: 68.2 us; the launch traced here: 68.1 us
  Pallas kernels  67.3 us (99%)
  between operations  0.8 us (1%)
    pallas_call x1, Pallas kernels, shards(): pl.pallas_call(functools.partial(kernel, rows_n, cols_n), out_shape=shape...  65.3 us
    pallas_call x1, Pallas kernels, shards(): pl.pallas_call(hand_over, out_shape=shapes, in_specs=[hbm] * 2, out_specs...  2.04 us

profile of v3, /device:TPU:1, one launch (start us, length us, event | category | flops | bytes accessed | tf_op | source)
XLA Modules:
  0.0 68.1 jit_solution(8461758739038492505)
XLA Ops:
  0.6 65.3 %shard_map.86 = (bf16[1024,512]{1,0:T(8,128)(2,1)}, bf16[64,512]{1,0:T(8,128)(2,1)}) custom-call(bf16[1024,512]{1,0:T(8,128)(2,1)} %bitcast.6, s32[1,1024]{1,0:T(1,128)} %bitcast.10, s32[8,128]{1,0:T(8,128)} %bitcast.11, bf16[64,512]{1,0:T(8,128)(2,1)} %bitcast.8, bf16[2,1536,512]{2,1,0:T(8,128)(2,1)} %w_in_hbm.1, bf16[2,2,2,512,512]{4,3,2,1,0:T(8,128)(2,1)} %w_res_hbm.1, ...), custom_call_target="tpu_custom_call" | custom-call | flops 11000000512 | bytes 12000000 | tf_op jit(solution)/shard_map/pallas_call | solution.py:352
  65.9 2.0 %shard_map.87 = (bf16[1024,512]{1,0:T(8,128)(2,1)}, bf16[64,512]{1,0:T(8,128)(2,1)}) custom-call(bf16[1024,512]{1,0:T(8,128)(2,1)} %get-tuple-element.6.edge_in, bf16[64,512]{1,0:T(8,128)(2,1)} %get-tuple-element.7.node_in), custom_call_target="tpu_custom_call" | custom-call | tf_op jit(solution)/shard_map/pallas_call | solution.py:396

commit v4 on v3

--- a/solution.py
+++ b/solution.py
@@ -159,19 +159,19 @@
         return pltpu.make_async_remote_copy(
             src_ref=u_out.at[t, b],
             dst_ref=u_in.at[t, (b ^ 1) - 2],
-            send_sem=col_send.at[t, b - 2],
-            recv_sem=col_recv.at[t, (b ^ 1) - 2],
+            send_sem=col_send.at[t, b // 2],
+            recv_sem=col_recv.at[t, b // 2],
             device_id=(r, col_peer(OFFSETS[b])),
             device_id_type=MESH,
         )
 
-    def col_arrival(t, k):
-        return pltpu.make_async_remote_copy(
-            src_ref=u_out.at[t, k],
-            dst_ref=u_in.at[t, k - 2],
-            send_sem=col_send.at[t, k - 2],
-            recv_sem=col_recv.at[t, k - 2],
-            device_id=(r, col_peer(OFFSETS[k])),
+    def col_both(t, q):
+        return pltpu.make_async_remote_copy(
+            src_ref=u_out.at[t, pl.ds(2 * q, 2)],
+            dst_ref=u_in.at[t, pl.ds(2 * q - 2, 2)],
+            send_sem=col_send.at[t, q],
+            recv_sem=col_recv.at[t, q],
+            device_id=(r, col_peer(OFFSETS[2 * q])),
             device_id_type=MESH,
         )
 
@@ -277,20 +277,16 @@
             rs_all(t, part).wait_send()
             ag_all(t, part).wait_send()
         if t:
-            for b in blocks_of(ORDER[-1]):
-                col_copy(t - 1, b).wait_send()
+            col_both(t - 1, ORDER[-1]).wait_send()
         for n, q in enumerate(ORDER):
             if n > 1:
-                for b in blocks_of(ORDER[n - 1]):
-                    col_copy(t, b).wait_send()
+                col_both(t, ORDER[n - 1]).wait_send()
             rows = pl.ds(q * pair, pair)
             arrived = []
+            if q:
+                col_both(t, q).wait_recv()
             for k in (2 * q, 2 * q + 1):
-                if q:
-                    col_arrival(t, k).wait_recv()
-                    arrived.append(u_in[t, k - 2])
-                else:
-                    arrived.append(u_out[t, k ^ 1])
+                arrived.append(u_in[t, k - 2] if q else u_out[t, k ^ 1])
             sums = pre[rows] + jnp.concatenate(arrived, axis=0).astype(F32)
             cur[rows] = edge_layer(sums, held[rows])
             if last:
@@ -311,8 +307,7 @@
                 else:
                     acc[points_of] = sums
 
-    for b in blocks_of(ORDER[-1]):
-        col_copy(layers - 1, b).wait_send()
+    col_both(layers - 1, ORDER[-1]).wait_send()
     for copy in edge_copies:
         copy.wait()
     node_copy.wait()
@@ -381,8 +376,8 @@
             dma((layers, PARTS)),
             dma((layers, PARTS)),
             dma((layers, PARTS)),
-            dma((layers, blocks - 2)),
-            dma((layers, blocks - 2)),
+            dma((layers, blocks // 2)),
+            dma((layers, blocks // 2)),
             dma((4,)),
             dma((blocks // 2 + 1,)),
         ],

time: 68.2 us -> 67.7 us (level)
  no operation moved by 1% of the time
where the time goes in v4:
time: 67.7 us; the launch traced here: 67.5 us
  Pallas kernels  66.7 us (99%)
  between operations  0.8 us (1%)
    pallas_call x1, Pallas kernels, shards(): pl.pallas_call(functools.partial(kernel, rows_n, cols_n), out_shape=shape...  64.7 us
    pallas_call x1, Pallas kernels, shards(): pl.pallas_call(hand_over, out_shape=shapes, in_specs=[hbm] * 2, out_specs...  2.04 us

profile of v4, /device:TPU:1, one launch (start us, length us, event | category | flops | bytes accessed | tf_op | source)
XLA Modules:
  0.0 67.5 jit_solution(9213115211136373110)
XLA Ops:
  0.6 64.7 %shard_map.86 = (bf16[1024,512]{1,0:T(8,128)(2,1)}, bf16[64,512]{1,0:T(8,128)(2,1)}) custom-call(bf16[1024,512]{1,0:T(8,128)(2,1)} %bitcast.6, s32[1,1024]{1,0:T(1,128)} %bitcast.10, s32[8,128]{1,0:T(8,128)} %bitcast.11, bf16[64,512]{1,0:T(8,128)(2,1)} %bitcast.8, bf16[2,1536,512]{2,1,0:T(8,128)(2,1)} %w_in_hbm.1, bf16[2,2,2,512,512]{4,3,2,1,0:T(8,128)(2,1)} %w_res_hbm.1, ...), custom_call_target="tpu_custom_call" | custom-call | flops 11000000512 | bytes 12000000 | tf_op jit(solution)/shard_map/pallas_call | solution.py:347
  65.3 2.0 %shard_map.87 = (bf16[1024,512]{1,0:T(8,128)(2,1)}, bf16[64,512]{1,0:T(8,128)(2,1)}) custom-call(bf16[1024,512]{1,0:T(8,128)(2,1)} %get-tuple-element.6.edge_in, bf16[64,512]{1,0:T(8,128)(2,1)} %get-tuple-element.7.node_in), custom_call_target="tpu_custom_call" | custom-call | tf_op jit(solution)/shard_map/pallas_call | solution.py:391

commit v5 on v4

--- a/solution.py
+++ b/solution.py
@@ -98,18 +98,18 @@
     def rows_of(device, part):
         return pl.ds(pl.multiple_of(device * share + part * piece, piece), piece)
 
-    barrier = pltpu.get_barrier_semaphore()
-    for j in range(others):
-        pl.semaphore_signal(barrier, inc=1, device_id=(row_peer(j), c), device_id_type=MESH)
-    for off in OFFSETS[2:]:
-        pl.semaphore_signal(barrier, inc=1, device_id=(r, col_peer(off)), device_id_type=MESH)
-
     firsts = []
     for i, (src, dst) in enumerate(
         ((tgt_hbm, tgt), (msg_hbm, msg), (rev_hbm, rev), (node_hbm, h_own))
     ):
         firsts.append(pltpu.make_async_copy(src, dst, in_sem.at[i]))
         firsts[-1].start()
+    barrier = pltpu.get_barrier_semaphore()
+    for j in range(others):
+        pl.semaphore_signal(barrier, inc=1, device_id=(row_peer(j), c), device_id_type=MESH)
+    for off in OFFSETS[2:]:
+        pl.semaphore_signal(barrier, inc=1, device_id=(r, col_peer(off)), device_id_type=MESH)
+
     def rs_copy(t, part, j):
         return pltpu.make_async_remote_copy(
             src_ref=part_out.at[t, part, j],

time: 67.7 us -> 67.7 us (level)
  no operation moved by 1% of the time
where the time goes in v5:
time: 67.7 us; the launch traced here: 67.6 us
  Pallas kernels  66.8 us (99%)
  between operations  0.8 us (1%)
    pallas_call x1, Pallas kernels, shards(): pl.pallas_call(functools.partial(kernel, rows_n, cols_n), out_shape=shape...  64.8 us
    pallas_call x1, Pallas kernels, shards(): pl.pallas_call(hand_over, out_shape=shapes, in_specs=[hbm] * 2, out_specs...  2.04 us

profile of v5, /device:TPU:1, one launch (start us, length us, event | category | flops | bytes accessed | tf_op | source)
XLA Modules:
  0.0 67.6 jit_solution(1752749336669934450)
XLA Ops:
  0.6 64.8 %shard_map.86 = (bf16[1024,512]{1,0:T(8,128)(2,1)}, bf16[64,512]{1,0:T(8,128)(2,1)}) custom-call(bf16[1024,512]{1,0:T(8,128)(2,1)} %bitcast.6, s32[1,1024]{1,0:T(1,128)} %bitcast.10, s32[8,128]{1,0:T(8,128)} %bitcast.11, bf16[64,512]{1,0:T(8,128)(2,1)} %bitcast.8, bf16[2,1536,512]{2,1,0:T(8,128)(2,1)} %w_in_hbm.1, bf16[2,2,2,512,512]{4,3,2,1,0:T(8,128)(2,1)} %w_res_hbm.1, ...), custom_call_target="tpu_custom_call" | custom-call | flops 11000000512 | bytes 12000000 | tf_op jit(solution)/shard_map/pallas_call | solution.py:347
  65.4 2.0 %shard_map.87 = (bf16[1024,512]{1,0:T(8,128)(2,1)}, bf16[64,512]{1,0:T(8,128)(2,1)}) custom-call(bf16[1024,512]{1,0:T(8,128)(2,1)} %get-tuple-element.6.edge_in, bf16[64,512]{1,0:T(8,128)(2,1)} %get-tuple-element.7.node_in), custom_call_target="tpu_custom_call" | custom-call | tf_op jit(solution)/shard_map/pallas_call | solution.py:391
